TPU v7x, 256 devices: a whole 4x4x8 slice. The times are simulated.
256 devices in a mesh: dom: 32 (over y, x, core), blk: 8 (over z).
Axes of the slice: x: 4, y: 4, z: 8, core: 2. Of those that a mesh axis runs over, the one named last changes fastest.
Arguments:
- source: bfloat16 [4096, 192], P(('dom', 'blk')), may hold values from -6 to 6
- lam_init: bfloat16 [4096, 192], P(('dom', 'blk')), may hold values from -6 to 6
- offd: bfloat16 [4096, 192, 1152], P(('dom', 'blk')), may hold values from -0.1875 to 0.1875
- dinv: bfloat16 [192, 786432], P(None, ('dom', 'blk')), may hold values from -0.4375 to 0.4375
- colidx: int32 [4096, 6], P(('dom', 'blk')), may hold values from 0 to 191
- face_list: int32 [32, 64], P('dom'), may hold values from 0 to 127
- partner: int32 [32], P('dom'), may hold values from 0 to 31, as said below
- perf_block: int32 [32768], P(('dom', 'blk')), may hold values from 0 to 15
- perf_well: int32 [32768], P(('dom', 'blk')), may hold values from 0 to 63
- perf_sens: bfloat16 [32768, 192], P(('dom', 'blk')), may hold values from -0.21875 to 0.21875
- obj_weight: float32 [1024], replicated, may hold values from 0.5 to 2
- step_index: int32 [1], replicated, may hold values from 0 to 1023
Outputs:
- adjoint: float32 [4096, 192], P(('dom', 'blk'))
- control_grad: float32 [2048], P(('dom', 'blk'))
Inputs may be any that keep to these rules, and one draw needn't show every extreme that they name: Below 128 an own block of the partition, from 128 on halo block colidx - 128. `face_list`: blocks of the partition's own 128, repeats possible. A pairing: partner[p] != p and partner[partner[p]] == p.
All inputs are finite; a program needn't handle non-finite values.
Results may differ from a plain program's by a relative error of at most 0.0054.
Values may be sent and summed in bfloat16 or wider, within the bound.
No kernel may reach another device: no remote copies, remote signals or barrier semaphores. Data moves between devices by JAX's collectives and lax.ppermute only.
A program may use at most 64 MiB of HBM per device.

v0:
```python
import jax
import jax.numpy as jnp
from jax import lax
from jax.sharding import PartitionSpec as P

WP = 64


def cross_partition(face_rows, partner_id):
    slot_count = lax.axis_size("dom")
    onehot = (jnp.arange(slot_count, dtype=jnp.int32) == partner_id).astype(jnp.bfloat16)
    outgoing = onehot[:, None, None] * face_rows[None, :, :]
    incoming = lax.all_to_all(outgoing, "dom", split_axis=0, concat_axis=0, tiled=True)
    halo_blocks = lax.dynamic_index_in_dim(incoming, partner_id, 0, keepdims=False)
    return halo_blocks


def extended_state(state, face_index, partner_id):
    partition = lax.all_gather(state, "blk", axis=0, tiled=True)
    halo_blocks = cross_partition(partition[face_index], partner_id)
    return jnp.concatenate([partition, halo_blocks], axis=0)


def sweep_once(state, forcing, offd, inverses, colidx, face_index, partner_id):
    extended = extended_state(state, face_index, partner_id)
    picked = extended[colidx].reshape(colidx.shape[0], -1)
    coupled = jnp.einsum("bim,bm->bi", offd, picked, preferred_element_type=jnp.float32)
    residual_rhs = (forcing - coupled).astype(jnp.bfloat16)
    return jnp.einsum("ibj,bj->bi", inverses, residual_rhs, preferred_element_type=jnp.float32)


def body(
    source,
    lam_init,
    offd,
    dinv,
    colidx,
    face_list,
    partner,
    perf_block,
    perf_well,
    perf_sens,
    obj_weight,
    step_index,
):
    weight = lax.dynamic_index_in_dim(obj_weight, step_index[0], 0, keepdims=False)
    forcing = weight * source.astype(jnp.float32)
    width = source.shape[1]
    inverses = dinv.reshape(width, source.shape[0], width)
    face_index = face_list[0]
    partner_id = partner[0]
    first_pass = sweep_once(
        lam_init, forcing, offd, inverses, colidx, face_index, partner_id
    ).astype(jnp.bfloat16)
    adjoint = sweep_once(first_pass, forcing, offd, inverses, colidx, face_index, partner_id)
    contrib = jnp.sum(perf_sens.astype(jnp.float32) * adjoint[perf_block], axis=1)
    onehot = (perf_well[:, None] == jnp.arange(WP, dtype=jnp.int32)[None, :]).astype(jnp.float32)
    well_terms = -jnp.dot(contrib, onehot, precision=lax.Precision.HIGHEST)
    control_grad = lax.psum_scatter(well_terms, "blk", scatter_dimension=0, tiled=True)
    return (adjoint, control_grad)


def solution(mesh):
    placed = (
        P(("dom", "blk"), None),
        P(("dom", "blk"), None),
        P(("dom", "blk"), None, None),
        P(None, ("dom", "blk")),
        P(("dom", "blk"), None),
        P("dom", None),
        P("dom"),
        P(("dom", "blk")),
        P(("dom", "blk")),
        P(("dom", "blk"), None),
        P(),
        P(),
    )
    return jax.shard_map(
        body,
        mesh=mesh,
        in_specs=placed,
        out_specs=(P(("dom", "blk"), None), P(("dom", "blk"))),
        check_vma=False,
    )
```

profile of v0, /device:TPU:2, one launch (start us, length us, event | category | flops | bytes accessed | tf_op | source)
XLA Modules:
  0.0 136.8 jit_solution(17076358415785166185)
XLA Ops:
  1.3 28.4 %all_gather.6 = bf16[128,192]{1,0:T(8,128)(2,1)S(1)} all-gather(bf16[16,192]{1,0:T(8,128)(2,1)} %param.13), channel_id=1, replica_groups=mesh['dom'=32,'blk'=8] {'blk'}, dimensions={0}, use_global_device_ids=true | all-gather | bytes 55296 | tf_op jit(solution)/shard_map/all_gather | solution.py:19
  29.7 0.7 fusion.10
  30.3 0.7 gather_fusion
  31.0 0.0 copy-start.4
  31.1 0.0 copy-start.1
  31.1 1.2 broadcast_multiply_fusion.1
  32.2 7.7 %all-to-all-start = ((bf16[32,64,192]{2,1,0:T(8,128)(2,1)}), bf16[32,64,192]{2,1,0:T(8,128)(2,1)}, u32[]{:S(2)}, u32[]{:S(2)}) async-start(bf16[32,64,192]{2,1,0:T(8,128)(2,1)} %broadcast_multiply_fusion.1), calls=%async_computation | async-start | bytes 2097152 | tf_op jit(solution)/shard_map/all_to_all | solution.py:13
  39.9 0.0 copy-done.4
  40.0 0.1 copy.18
  40.0 0.1 reshape.62
  40.8 0.0 copy-done.1
  40.8 0.7 copy.29
  41.5 1.3 dynamic_slice.11
  42.8 13.3 %all-to-all-done = bf16[32,64,192]{2,1,0:T(8,128)(2,1)} async-done(((bf16[32,64,192]{2,1,0:T(8,128)(2,1)}), bf16[32,64,192]{2,1,0:T(8,128)(2,1)}, u32[]{:S(2)}, u32[]{:S(2)}) %all-to-all-start) | async-done | bytes 786464 | tf_op jit(solution)/shard_map/all_to_all | solution.py:13
  56.1 0.8 dynamic-slice_bitcast_fusion.1
  56.9 0.8 gather_fusion.1
  57.7 0.1 reshape.110
  57.8 0.0 copy-start.3
  57.8 5.2 %fusion.12 = f32[16,1,192]{2,1,0:T(1,128)S(1)} fusion(bf16[16,1152,1]{1,2,0:T(2,128)(2,1)S(1)} %reshape.110, bf16[16,192,1152]{2,1,0:T(8,128)(2,1)} %param.14), kind=kOutput, calls=%fused_computation.38 | convolution fusion | flops 7077888 | bytes 7127040 | tf_op jit(solution)/shard_map/bim,bm->bi/dot_general | solution.py:27
  62.9 0.0 copy-done.3
  62.9 0.7 fusion.8
  63.6 0.3 fusion.6
  63.9 24.6 %all_gather.7 = bf16[128,192]{1,0:T(8,128)(2,1)S(1)} all-gather(bf16[16,192]{1,0:T(8,128)(2,1)S(1)} %bitcast.59), channel_id=1, replica_groups=mesh['dom'=32,'blk'=8] {'blk'}, dimensions={0}, use_global_device_ids=true | all-gather | bytes 55296 | tf_op jit(solution)/shard_map/all_gather | solution.py:19
  88.5 0.7 gather_fusion.2
  89.2 0.0 copy-start.2
  89.2 0.0 copy-start.7
  89.2 0.0 copy-start.5
  89.2 1.1 broadcast_multiply_fusion
  90.3 5.0 %all-to-all-start.1 = ((bf16[32,64,192]{2,1,0:T(8,128)(2,1)}), bf16[32,64,192]{2,1,0:T(8,128)(2,1)S(1)}, u32[]{:S(2)}, u32[]{:S(2)}) async-start(bf16[32,64,192]{2,1,0:T(8,128)(2,1)} %broadcast_multiply_fusion), calls=%async_computation.1 | async-start | bytes 2097152 | tf_op jit(solution)/shard_map/all_to_all | solution.py:13
  95.4 0.0 copy-done.2
  95.4 0.1 copy.19
  95.5 0.0 copy-done.7
  95.5 0.6 dynamic-slice
  96.8 0.0 copy-done.5
  96.8 14.8 %all-to-all-done.1 = bf16[32,64,192]{2,1,0:T(8,128)(2,1)S(1)} async-done(((bf16[32,64,192]{2,1,0:T(8,128)(2,1)}), bf16[32,64,192]{2,1,0:T(8,128)(2,1)S(1)}, u32[]{:S(2)}, u32[]{:S(2)}) %all-to-all-start.1) | async-done | bytes 786464 | tf_op jit(solution)/shard_map/all_to_all | solution.py:13
  111.6 0.8 gather_fusion.3
  112.4 0.1 reshape.112
  112.5 5.2 %fusion.13 = f32[16,1,192]{2,1,0:T(1,128)S(1)} fusion(bf16[16,1152,1]{1,2,0:T(2,128)(2,1)S(1)} %reshape.112, bf16[16,192,1152]{2,1,0:T(8,128)(2,1)} %param.14), kind=kOutput, calls=%fused_computation.39 | convolution fusion | flops 7077888 | bytes 7127040 | tf_op jit(solution)/shard_map/bim,bm->bi/dot_general | solution.py:27
  117.7 0.0 copy-start.6
  117.7 0.7 fusion.9
  118.4 0.3 fusion.4
  118.7 0.8 gather_fusion.4
  119.5 0.1 multiply_reduce_fusion
  119.6 0.0 copy-done.6
  119.6 0.2 fusion
  119.8 16.4 %all-reduce = f32[64]{0:T(128)S(1)} all-reduce(f32[64]{0:T(128)S(1)} %fusion), channel_id=2, replica_groups=mesh['dom'=32,'blk'=8] {'blk'}, use_global_device_ids=true, to_apply=%region_1.2.clone | all-reduce | flops 64 | bytes 512
  136.2 0.6 dynamic-slice.1
  136.8 0.0 copy-done
  (12 shorter events, 0.1 us)
Async XLA Ops:
  31.0 8.9 %copy-start.4 = (s32[16,6]{0,1:T(8,128)S(1)}, s32[16,6]{0,1:T(8,128)}, u32[]{:S(2)}) copy-start(s32[16,6]{0,1:T(8,128)} %param.16) | copy-start | bytes 1156
  31.1 9.7 %copy-start.1 = (bf16[192,3072]{1,0:T(8,128)(2,1)S(1)}, bf16[192,3072]{1,0:T(8,128)(2,1)}, u32[]{:S(2)}) copy-start(bf16[192,3072]{1,0:T(8,128)(2,1)} %param.15) | copy-start | bytes 3538948
  32.2 23.8 %all-to-all-start = ((bf16[32,64,192]{2,1,0:T(8,128)(2,1)}), bf16[32,64,192]{2,1,0:T(8,128)(2,1)}, u32[]{:S(2)}, u32[]{:S(2)}) async-start(bf16[32,64,192]{2,1,0:T(8,128)(2,1)} %broadcast_multiply_fusion.1), calls=%async_computation | async-start | bytes 2097152 | tf_op jit(solution)/shard_map/all_to_all | solution.py:13
  57.8 5.2 %copy-start.3 = (bf16[16,192]{1,0:T(8,128)(2,1)S(1)}, bf16[16,192]{1,0:T(8,128)(2,1)}, u32[]{:S(2)}) copy-start(bf16[16,192]{1,0:T(8,128)(2,1)} %param.12) | copy-start | bytes 18436
  89.2 6.2 %copy-start.2 = (bf16[128,192]{0,1:T(8,128)(2,1)S(1)}, bf16[128,192]{0,1:T(8,128)(2,1)}, u32[]{:S(2)}) copy-start(bf16[128,192]{0,1:T(8,128)(2,1)} %param.21) | copy-start | bytes 147460
  89.2 6.3 %copy-start.7 = (u32[256]{0:T(256)S(1)}, u32[256]{0:T(256)}, u32[]{:S(2)}) copy-start(u32[256]{0:T(256)} %constant.35) | copy-start | bytes 3076
  89.2 7.6 %copy-start.5 = (s32[128]{0:T(128)S(1)}, s32[128]{0:T(128)}, u32[]{:S(2)}) copy-start(s32[128]{0:T(128)} %param.19) | copy-start | bytes 1540
  90.3 21.3 %all-to-all-start.1 = ((bf16[32,64,192]{2,1,0:T(8,128)(2,1)}), bf16[32,64,192]{2,1,0:T(8,128)(2,1)S(1)}, u32[]{:S(2)}, u32[]{:S(2)}) async-start(bf16[32,64,192]{2,1,0:T(8,128)(2,1)} %broadcast_multiply_fusion), calls=%async_computation.1 | async-start | bytes 2097152 | tf_op jit(solution)/shard_map/all_to_all | solution.py:13
  117.7 1.9 %copy-start.6 = (s32[128]{0:T(128)S(1)}, s32[128]{0:T(128)}, u32[]{:S(2)}) copy-start(s32[128]{0:T(128)} %param.20) | copy-start | bytes 1540
  118.7 18.1 %copy-start = (f32[16,1,192]{2,0,1:T(8,128)}, f32[16,1,192]{2,0,1:T(8,128)S(1)}, u32[]{:S(2)}) copy-start(f32[16,1,192]{2,0,1:T(8,128)S(1)} %copy.43) | copy-start | bytes 36868
where the time goes:
time: 137 us
  blocking collectives  69.3 us (51%)
  waiting for transfers between devices  28.1 us (21%)
  starting transfers between devices  12.7 us (9%)
  matrix products  11.1 us (8%)
  local copies, waits for them, and re-layouts  8.15 us (6%)
  other arithmetic  4.47 us (3%)
  between operations  2.83 us (2%)
    all_gather x2, blocking collectives, extended_state(): partition = lax.all_gather(state, 'blk', axis=0, tiled=True)  52.9 us
    all_to_all x2, waiting for transfers between devices, cross_partition(): lax.all_to_all(outgoing, 'dom', split_axis=0, concat_axis=0, tiled=True)  28.1 us
    unnamed x1, blocking collectives  16.4 us
    all_to_all x2, starting transfers between devices, cross_partition(): lax.all_to_all(outgoing, 'dom', split_axis=0, concat_axis=0, tiled=True)  12.7 us
    dot_general x2, matrix products, sweep_once(): jnp.einsum('bim,bm->bi', offd, picked, preferred_element_type=jnp.float32)  10.3 us
  transfers between devices with their start and end apart: 2, of which 2 were waited for; matrix products, arithmetic and copies ran while one was open for 2% of the time, Pallas kernels for 0%

commit v1 on v0

--- a/solution.py
+++ b/solution.py
@@ -2,6 +2,7 @@
 import jax.numpy as jnp
 from jax import lax
 from jax.sharding import PartitionSpec as P
+from jax.lax import all_to_all, axis_size
 
 WP = 64
 
@@ -16,7 +17,15 @@
 
 
 def extended_state(state, face_index, partner_id):
-    partition = lax.all_gather(state, "blk", axis=0, tiled=True)
+    partition = jnp.concatenate(
+        all_to_all(
+            jnp.stack(tuple((state for _ in range(axis_size("blk")))), axis=0),
+            axis_name="blk",
+            split_axis=0,
+            concat_axis=0,
+        ),
+        axis=0,
+    )
     halo_blocks = cross_partition(partition[face_index], partner_id)
     return jnp.concatenate([partition, halo_blocks], axis=0)
 

time: 137 us -> 111 us (0.81)
  blocking collectives: 69.3 us -> 25.5 us
  starting transfers between devices: 12.7 us -> 21.2 us
  waiting for transfers between devices: 28.1 us -> 35.2 us
    all_gather x2 -> x0, blocking collectives: 52.9 us -> none  [extended_state(): partition = lax.all_gather(state, 'blk', axis=0, tiled=True)]
    all_to_all x0 -> x1, blocking collectives: none -> 10.8 us  [extended_state(): all_to_all(jnp.stack(tuple((state for _ in range(axis_size('blk')))), axi...]
    all_to_all x0 -> x1, starting transfers between devices: none -> 8.47 us  [extended_state(): all_to_all(jnp.stack(tuple((state for _ in range(axis_size('blk')))), axi...]
    all_to_all x0 -> x1, waiting for transfers between devices: none -> 7.05 us  [extended_state(): all_to_all(jnp.stack(tuple((state for _ in range(axis_size('blk')))), axi...]
    unnamed x1, blocking collectives: 16.4 us -> 14.7 us
  transfers between devices with their start and end apart: 2 -> 3, of which waited for: 2 -> 3; matrix products, arithmetic and copies ran while one was open for 2% -> 3% of each run, Pallas kernels for 0% -> 0%
where the time goes in v1:
time: 111 us; the launch traced here: 110 us
  waiting for transfers between devices  35.2 us (32%)
  blocking collectives  25.5 us (23%)
  starting transfers between devices  21.2 us (19%)
  matrix products  11.1 us (10%)
  local copies, waits for them, and re-layouts  9.49 us (9%)
  other arithmetic  4.46 us (4%)
  between operations  2.83 us (3%)
    all_to_all x2, waiting for transfers between devices, cross_partition(): lax.all_to_all(outgoing, 'dom', split_axis=0, concat_axis=0, tiled=True)  28.1 us
    unnamed x1, blocking collectives  14.7 us
    all_to_all x2, starting transfers between devices, cross_partition(): lax.all_to_all(outgoing, 'dom', split_axis=0, concat_axis=0, tiled=True)  12.7 us
    all_to_all x1, blocking collectives, extended_state(): all_to_all(jnp.stack(tuple((state for _ in range(axis_size('blk')))), axi...  10.8 us
    dot_general x2, matrix products, sweep_once(): jnp.einsum('bim,bm->bi', offd, picked, preferred_element_type=jnp.float32)  10.3 us
    all_to_all x1, starting transfers between devices, extended_state(): all_to_all(jnp.stack(tuple((state for _ in range(axis_size('blk')))), axi...  8.47 us
    all_to_all x1, waiting for transfers between devices, extended_state(): all_to_all(jnp.stack(tuple((state for _ in range(axis_size('blk')))), axi...  7.05 us
    mul x2, other arithmetic, cross_partition(): outgoing = onehot[:, None, None] * face_rows[None, :, :]  2.27 us
  transfers between devices with their start and end apart: 3, of which 3 were waited for; matrix products, arithmetic and copies ran while one was open for 3% of the time, Pallas kernels for 0%

profile of v1, /device:TPU:2, one launch (start us, length us, event | category | flops | bytes accessed | tf_op | source)
XLA Modules:
  0.0 109.8 jit_solution(6710811000102775525)
XLA Ops:
  0.6 1.3 %stack.4 = bf16[8,16,192]{2,1,0:T(8,128)(2,1)} broadcast(bf16[16,192]{1,0:T(8,128)(2,1)} %param.13), dimensions={1,2} | broadcast | bytes 55296 | tf_op jit(solution)/shard_map/stack | solution.py:22
  2.0 8.5 %all-to-all-start = ((bf16[8,16,192]{2,1,0:T(8,128)(2,1)}), bf16[8,16,192]{2,1,0:T(8,128)(2,1)S(1)}, u32[]{:S(2)}, u32[]{:S(2)}) async-start(bf16[8,16,192]{2,1,0:T(8,128)(2,1)} %stack.4), calls=%async_computation | async-start | bytes 131072 | tf_op jit(solution)/shard_map/all_to_all | solution.py:21
  11.1 0.7 fusion.10
  11.8 7.1 %all-to-all-done = bf16[8,16,192]{2,1,0:T(8,128)(2,1)S(1)} async-done(((bf16[8,16,192]{2,1,0:T(8,128)(2,1)}), bf16[8,16,192]{2,1,0:T(8,128)(2,1)S(1)}, u32[]{:S(2)}, u32[]{:S(2)}) %all-to-all-start) | async-done | bytes 49184 | tf_op jit(solution)/shard_map/all_to_all | solution.py:21
  18.8 0.7 gather_fusion
  19.5 0.0 copy-start.4
  19.5 0.0 copy-start.1
  19.5 1.2 %broadcast_multiply_fusion.1 = bf16[32,64,192]{2,1,0:T(8,128)(2,1)} fusion(bf16[64,192]{1,0:T(8,128)(2,1)S(1)} %gather_fusion, bf16[32]{0:T(256)(128)(2,1)S(1)} %compare_convert_fusion), kind=kLoop, calls=%fused_computation.8 | loop fusion | flops 393216 | bytes 811072 | tf_op jit(solution)/shard_map/mul | solution.py:13
  20.7 7.7 %all-to-all-start.1 = ((bf16[32,64,192]{2,1,0:T(8,128)(2,1)}), bf16[32,64,192]{2,1,0:T(8,128)(2,1)}, u32[]{:S(2)}, u32[]{:S(2)}) async-start(bf16[32,64,192]{2,1,0:T(8,128)(2,1)} %broadcast_multiply_fusion.1), calls=%async_computation.1 | async-start | bytes 2097152 | tf_op jit(solution)/shard_map/all_to_all | solution.py:14
  28.4 0.0 copy-done.4
  28.4 0.1 copy.18
  28.5 0.1 reshape.74
  29.2 0.0 copy-done.1
  29.2 0.7 copy.29
  29.9 1.3 %dynamic_slice.11 = f32[1]{0:T(128)} dynamic-slice(f32[1024]{0:T(1024)} %param.22, s32[]{:T(128)S(6)} %select_n.27), dynamic_slice_sizes={1} | dynamic-slice | bytes 12 | tf_op jit(solution)/shard_map/jit(dynamic_index_in_dim)/dynamic_slice | solution.py:55
  31.2 13.3 %all-to-all-done.1 = bf16[32,64,192]{2,1,0:T(8,128)(2,1)} async-done(((bf16[32,64,192]{2,1,0:T(8,128)(2,1)}), bf16[32,64,192]{2,1,0:T(8,128)(2,1)}, u32[]{:S(2)}, u32[]{:S(2)}) %all-to-all-start.1) | async-done | bytes 786464 | tf_op jit(solution)/shard_map/all_to_all | solution.py:14
  44.5 0.8 dynamic-slice_bitcast_fusion.1
  45.3 0.8 gather_fusion.1
  46.1 0.1 reshape.122
  46.2 0.0 copy-start.3
  46.2 5.2 %fusion.12 = f32[16,1,192]{2,1,0:T(1,128)S(1)} fusion(bf16[16,1152,1]{1,2,0:T(2,128)(2,1)S(1)} %reshape.122, bf16[16,192,1152]{2,1,0:T(8,128)(2,1)} %param.14), kind=kOutput, calls=%fused_computation.38 | convolution fusion | flops 7077888 | bytes 7127040 | tf_op jit(solution)/shard_map/bim,bm->bi/dot_general | solution.py:36
  51.4 0.0 copy-done.3
  51.4 0.7 fusion.8
  52.1 0.3 fusion.6
  52.4 10.8 %all_to_all.20 = bf16[8,16,192]{2,1,0:T(8,128)(2,1)S(1)} all-to-all(bf16[8,16,192]{2,1,0:T(8,128)(2,1)S(1)} %stack.5), channel_id=1, replica_groups=mesh['dom'=32,'blk'=8] {'blk'}, dimensions={0} | all-to-all | bytes 98304 | tf_op jit(solution)/shard_map/all_to_all | solution.py:21
  63.2 0.7 gather_fusion.2
  63.9 0.0 copy-start.2
  63.9 0.0 copy-start.7
  63.9 0.0 copy-start.5
  63.9 1.1 %broadcast_multiply_fusion = bf16[32,64,192]{2,1,0:T(8,128)(2,1)} fusion(bf16[64,192]{1,0:T(8,128)(2,1)S(1)} %gather_fusion.2, bf16[32]{0:T(256)(128)(2,1)S(1)} %compare_convert_fusion), kind=kLoop, calls=%fused_computation.7 | loop fusion | flops 393216 | bytes 811072 | tf_op jit(solution)/shard_map/mul | solution.py:13
  65.0 5.0 %all-to-all-start.3 = ((bf16[32,64,192]{2,1,0:T(8,128)(2,1)}), bf16[32,64,192]{2,1,0:T(8,128)(2,1)S(1)}, u32[]{:S(2)}, u32[]{:S(2)}) async-start(bf16[32,64,192]{2,1,0:T(8,128)(2,1)} %broadcast_multiply_fusion), calls=%async_computation.3 | async-start | bytes 2097152 | tf_op jit(solution)/shard_map/all_to_all | solution.py:14
  70.1 0.0 copy-done.2
  70.1 0.1 copy.19
  70.2 0.0 copy-done.7
  70.2 0.6 dynamic-slice
  71.4 0.0 copy-done.5
  71.5 14.8 %all-to-all-done.3 = bf16[32,64,192]{2,1,0:T(8,128)(2,1)S(1)} async-done(((bf16[32,64,192]{2,1,0:T(8,128)(2,1)}), bf16[32,64,192]{2,1,0:T(8,128)(2,1)S(1)}, u32[]{:S(2)}, u32[]{:S(2)}) %all-to-all-start.3) | async-done | bytes 786464 | tf_op jit(solution)/shard_map/all_to_all | solution.py:14
  86.3 0.8 gather_fusion.3
  87.1 0.1 reshape.124
  87.2 5.2 %fusion.13 = f32[16,1,192]{2,1,0:T(1,128)S(1)} fusion(bf16[16,1152,1]{1,2,0:T(2,128)(2,1)S(1)} %reshape.124, bf16[16,192,1152]{2,1,0:T(8,128)(2,1)} %param.14), kind=kOutput, calls=%fused_computation.39 | convolution fusion | flops 7077888 | bytes 7127040 | tf_op jit(solution)/shard_map/bim,bm->bi/dot_general | solution.py:36
  92.3 0.7 fusion.9
  93.0 0.3 fusion.4
  93.4 0.8 gather_fusion.4
  94.1 0.1 multiply_reduce_fusion
  94.2 0.0 copy-done.6
  94.2 0.2 fusion
  94.4 14.7 %all-reduce = f32[64]{0:T(128)S(1)} all-reduce(f32[64]{0:T(128)S(1)} %fusion), channel_id=2, replica_groups=mesh['dom'=32,'blk'=8] {'blk'}, use_global_device_ids=true, to_apply=%region_1.2.clone | all-reduce | flops 64 | bytes 512
  109.2 0.6 dynamic-slice.1
  (15 shorter events, 0.1 us)
Async XLA Ops:
  2.0 16.8 %all-to-all-start = ((bf16[8,16,192]{2,1,0:T(8,128)(2,1)}), bf16[8,16,192]{2,1,0:T(8,128)(2,1)S(1)}, u32[]{:S(2)}, u32[]{:S(2)}) async-start(bf16[8,16,192]{2,1,0:T(8,128)(2,1)} %stack.4), calls=%async_computation | async-start | bytes 131072 | tf_op jit(solution)/shard_map/all_to_all | solution.py:21
  19.5 8.9 %copy-start.4 = (s32[16,6]{0,1:T(8,128)S(1)}, s32[16,6]{0,1:T(8,128)}, u32[]{:S(2)}) copy-start(s32[16,6]{0,1:T(8,128)} %param.16) | copy-start | bytes 1156
  19.5 9.7 %copy-start.1 = (bf16[192,3072]{1,0:T(8,128)(2,1)S(1)}, bf16[192,3072]{1,0:T(8,128)(2,1)}, u32[]{:S(2)}) copy-start(bf16[192,3072]{1,0:T(8,128)(2,1)} %param.15) | copy-start | bytes 3538948
  20.7 23.8 %all-to-all-start.1 = ((bf16[32,64,192]{2,1,0:T(8,128)(2,1)}), bf16[32,64,192]{2,1,0:T(8,128)(2,1)}, u32[]{:S(2)}, u32[]{:S(2)}) async-start(bf16[32,64,192]{2,1,0:T(8,128)(2,1)} %broadcast_multiply_fusion.1), calls=%async_computation.1 | async-start | bytes 2097152 | tf_op jit(solution)/shard_map/all_to_all | solution.py:14
  46.2 5.2 %copy-start.3 = (bf16[16,192]{1,0:T(8,128)(2,1)S(1)}, bf16[16,192]{1,0:T(8,128)(2,1)}, u32[]{:S(2)}) copy-start(bf16[16,192]{1,0:T(8,128)(2,1)} %param.12) | copy-start | bytes 18436
  63.9 6.2 %copy-start.2 = (bf16[128,192]{0,1:T(8,128)(2,1)S(1)}, bf16[128,192]{0,1:T(8,128)(2,1)}, u32[]{:S(2)}) copy-start(bf16[128,192]{0,1:T(8,128)(2,1)} %param.21) | copy-start | bytes 147460
  63.9 6.3 %copy-start.7 = (u32[256]{0:T(256)S(1)}, u32[256]{0:T(256)}, u32[]{:S(2)}) copy-start(u32[256]{0:T(256)} %constant.35) | copy-start | bytes 3076
  63.9 7.6 %copy-start.5 = (s32[128]{0:T(128)S(1)}, s32[128]{0:T(128)}, u32[]{:S(2)}) copy-start(s32[128]{0:T(128)} %param.19) | copy-start | bytes 1540
  65.0 21.3 %all-to-all-start.3 = ((bf16[32,64,192]{2,1,0:T(8,128)(2,1)}), bf16[32,64,192]{2,1,0:T(8,128)(2,1)S(1)}, u32[]{:S(2)}, u32[]{:S(2)}) async-start(bf16[32,64,192]{2,1,0:T(8,128)(2,1)} %broadcast_multiply_fusion), calls=%async_computation.3 | async-start | bytes 2097152 | tf_op jit(solution)/shard_map/all_to_all | solution.py:14
  92.3 1.9 %copy-start.6 = (s32[128]{0:T(128)S(1)}, s32[128]{0:T(128)}, u32[]{:S(2)}) copy-start(s32[128]{0:T(128)} %param.20) | copy-start | bytes 1540
  93.4 16.4 %copy-start = (f32[16,1,192]{2,0,1:T(8,128)}, f32[16,1,192]{2,0,1:T(8,128)S(1)}, u32[]{:S(2)}) copy-start(f32[16,1,192]{2,0,1:T(8,128)S(1)} %copy.43) | copy-start | bytes 36868
